TPU v7x, 32 devices: a whole 2x2x4 slice. The times are simulated.
32 devices in a mesh: groups: 2 (over y), dom: 4 (over z), mem: 2 (over x), sub: 2 (over core).
Axes of the slice: x: 2, y: 2, z: 4, core: 2. Of those that a mesh axis runs over, the one named last changes fastest.
Arguments:
- ensemble: float32 [32, 65536], P('mem', ('groups', 'dom', 'sub')), parts along dimension 1
- station_cells: int32 [2048, 4], P('groups'), parts along dimension 0, may hold values from 0 to 4095, as said below
- owners: int32 [2048], P('groups'), parts along dimension 0, may hold values from 0 to 7
- interp_weights: float32 [2048, 4], P('groups'), parts along dimension 0
- station_order: int32 [2048], P('groups'), parts along dimension 0, may hold values from 0 to 1023, each once
- obs_values: float32 [2048], P('groups'), parts along dimension 0, may hold values from -6 to 6
- obs_var: float32 [2048], P('groups'), parts along dimension 0, may hold values from 0.2 to 2
- partners: int32 [1024, 16], P(('groups', 'dom', 'sub')), parts along dimension 0, may hold values from 0 to 511, as said below
Outputs:
- analysis: float32 [32, 65536], P('mem', ('groups', 'dom', 'sub')), parts along dimension 1
There are 2 independent parts, one for each index of `groups`. A program takes and returns all parts, laid end to end along the dimension named above; each array names one. Nothing has to cross between parts.
Inputs may be any that keep to these rules, and one draw needn't show every extreme that they name: `station_cells`: the four cells of a station lie in one aligned block of 64 values. `partners`: each state block lists itself first; the other entries may repeat. `station_order`: a permutation of the stations.
All inputs are finite; a program needn't handle non-finite values.
Results may differ from a plain program's by a relative error of at most 0.0003.
Values sent between devices are 32-bit elements; how exact they have to be, the bound alone decides.
A program may use at most 64 MiB of HBM per device.

v0:
```python
import jax
import jax.numpy as jnp
from jax import lax
from jax.sharding import PartitionSpec as P

BLOCK = 64
P_SIZE = 256
NBATCH = 4


def increments(obs_prior, observed, noise_var):
    member_count = obs_prior.shape[0]
    mean_prior = jnp.mean(obs_prior, axis=0)
    spread = obs_prior - mean_prior[None, :]
    variance = jnp.sum(spread * spread, axis=0) / (member_count - 1)
    shrink_ratio = jnp.sqrt(noise_var / (variance + noise_var))
    posterior = (noise_var * mean_prior + variance * observed) / (variance + noise_var)
    obs_shift = (posterior - mean_prior)[None, :] + (shrink_ratio - 1.0)[None, :] * spread
    gain_factor = 1.0 / ((variance + 1e-05) * (member_count - 1))
    return (spread, obs_shift, gain_factor)


def local_gain(cross_cov, gain_scale):
    cell_count = cross_cov.shape[0]
    shaped = (
        cross_cov.reshape(cell_count // BLOCK, BLOCK, cross_cov.shape[1]) * gain_scale[:, None, :]
    )
    return shaped.reshape(cell_count, cross_cov.shape[1])


def body(
    ensemble, station_cells, owners, interp_weights, station_order, obs_values, obs_var, partners
):
    local_rows = ensemble.shape[0]
    my_width = ensemble.shape[1]
    blocks_dev = my_width // BLOCK
    member_count = local_rows * lax.axis_size("mem")
    me_part = lax.axis_index(("dom", "sub"))
    me_mem = lax.axis_index("mem")
    block_cells = my_width // 8
    current = ensemble
    for batch_index in range(NBATCH):
        picked = station_order[batch_index * P_SIZE : (batch_index + 1) * P_SIZE]
        owner_part = owners[picked]
        spot_cells = station_cells[picked]
        stat_block = owner_part * blocks_dev + spot_cells[:, 0] // BLOCK
        matches = partners[:, :, None] == stat_block[None, None, :]
        nearby = jnp.any(matches, axis=1).astype(jnp.float32)
        owner_part, spot_cells, interp, observed, noise_var, nearby = (
            owner_part,
            spot_cells,
            interp_weights[picked],
            obs_values[picked],
            obs_var[picked],
            nearby,
        )
        is_mine = (owner_part == me_part).astype(jnp.float32)
        local_prior = jnp.sum(current[:, spot_cells] * interp[None], axis=2) * is_mine[None, :]
        padded = jnp.zeros((member_count, P_SIZE), jnp.float32)
        padded = lax.dynamic_update_slice_in_dim(padded, local_prior, me_mem * local_rows, 0)
        obs_prior = lax.psum(padded, ("dom", "mem", "sub"))
        spread, obs_shift, gain_factor = increments(obs_prior, observed, noise_var)
        gain_scale = nearby * gain_factor[None, :]
        my_shift = lax.dynamic_slice_in_dim(obs_shift, me_mem * local_rows, local_rows, 0)

        def update(step_index, running_state):
            begin = step_index * block_cells
            cell_block = lax.dynamic_slice_in_dim(running_state, begin, block_cells, 1)
            all_members = lax.all_gather(cell_block, "mem", axis=0, tiled=True)
            cross_cov = jnp.einsum(
                "mc,mp->cp", all_members, spread, precision=lax.Precision.HIGHEST
            )
            block_scale = lax.dynamic_slice_in_dim(
                gain_scale, begin // BLOCK, block_cells // BLOCK, 0
            )
            gain_matrix = local_gain(cross_cov, block_scale)
            change = jnp.einsum("mp,cp->mc", my_shift, gain_matrix, precision=lax.Precision.HIGHEST)
            return lax.dynamic_update_slice_in_dim(running_state, cell_block + change, begin, 1)

        current = lax.fori_loop(0, 8, update, current)
    return current


def solution(mesh):
    return jax.shard_map(
        body,
        mesh=mesh,
        in_specs=(
            P("mem", ("groups", "dom", "sub")),
            P("groups", None),
            P("groups"),
            P("groups", None),
            P("groups"),
            P("groups"),
            P("groups"),
            P(("groups", "dom", "sub"), None),
        ),
        out_specs=P("mem", ("groups", "dom", "sub")),
        check_vma=False,
    )
```

profile of v0, /device:TPU:0, one launch (start us, length us, event | category | flops | bytes accessed | tf_op | source)
XLA Modules:
  0.0 468.1 jit_solution(6577044838444136825)
XLA Ops:
  30.9 62.9 %psum.28 = f32[32,256]{1,0:T(8,128)S(1)} all-reduce(f32[32,256]{1,0:T(8,128)S(1)} %constant_dynamic-update-slice_fusion.3), channel_id=1, replica_groups=mesh['groups'=2,'dom'=4,'mem'=2,'sub'=2] {'dom','mem','sub'}, use_global_device_ids=true, to_apply=%region_1.2 | all-reduce | flops 8192 | bytes 65536 | tf_op jit(solution)/shard_map/psum | solution.py:61
  93.9 47.0 %while.60 = (s32[]{:T(128)}, f32[16,4096]{1,0:T(8,128)S(1)}, f32[32,256]{1,0:T(8,128)S(1)}, f32[64,256]{1,0:T(8,128)S(1)}, f32[16,256]{1,0:T(8,128)S(1)}, /*inde...) while((s32[]{:T(128)}, f32[16,4096]{1,0:T(8,128)S(1)}, ...), condition=%wide.region_6.7_spmd, body=%wide.region_5.6_spmd.sunk | while | flops 75636760 | bytes 2466150 | solution.py:80
  94.0 4.6 all_gather.44
  99.9 4.6 all_gather.44
  105.7 4.6 all_gather.44
  111.6 4.6 all_gather.44
  117.5 4.6 all_gather.44
  123.3 4.6 all_gather.44
  129.2 4.6 all_gather.44
  135.1 4.6 all_gather.44
  144.9 57.6 %psum.29 = f32[32,256]{1,0:T(8,128)S(1)} all-reduce(f32[32,256]{1,0:T(8,128)S(1)} %constant_dynamic-update-slice_fusion.2), channel_id=1, replica_groups=mesh['groups'=2,'dom'=4,'mem'=2,'sub'=2] {'dom','mem','sub'}, use_global_device_ids=true, to_apply=%region_8.9 | all-reduce | flops 8192 | bytes 65536 | tf_op jit(solution)/shard_map/psum | solution.py:61
  202.7 47.0 %while.61 = (s32[]{:T(128)}, f32[16,4096]{1,0:T(8,128)S(1)}, f32[32,256]{1,0:T(8,128)S(1)}, f32[64,256]{1,0:T(8,128)S(1)}, f32[16,256]{1,0:T(8,128)S(1)}, /*inde...) while((s32[]{:T(128)}, f32[16,4096]{1,0:T(8,128)S(1)}, ...), condition=%wide.region_13.14_spmd, body=%wide.region_12.13_spmd.sunk | while | flops 75636760 | bytes 2466150 | solution.py:80
  202.8 4.6 all_gather.45
  208.6 4.6 all_gather.45
  214.5 4.6 all_gather.45
  220.4 4.6 all_gather.45
  226.2 4.6 all_gather.45
  232.1 4.6 all_gather.45
  238.0 4.6 all_gather.45
  253.7 57.8 %psum.30 = f32[32,256]{1,0:T(8,128)S(1)} all-reduce(f32[32,256]{1,0:T(8,128)S(1)} %constant_dynamic-update-slice_fusion.1), channel_id=1, replica_groups=mesh['groups'=2,'dom'=4,'mem'=2,'sub'=2] {'dom','mem','sub'}, use_global_device_ids=true, to_apply=%region_15.16 | all-reduce | flops 8192 | bytes 65536 | tf_op jit(solution)/shard_map/psum | solution.py:61
  311.6 47.0 %while.62 = (s32[]{:T(128)}, f32[16,4096]{1,0:T(8,128)S(1)}, f32[32,256]{1,0:T(8,128)S(1)}, f32[64,256]{1,0:T(8,128)S(1)}, f32[16,256]{1,0:T(8,128)S(1)}, /*inde...) while((s32[]{:T(128)}, f32[16,4096]{1,0:T(8,128)S(1)}, ...), condition=%wide.region_20.21_spmd, body=%wide.region_19.20_spmd.sunk | while | flops 75636760 | bytes 2466150 | solution.py:80
  311.7 4.6 all_gather.46
  362.7 57.6 %psum.31 = f32[32,256]{1,0:T(8,128)S(1)} all-reduce(f32[32,256]{1,0:T(8,128)S(1)} %constant_dynamic-update-slice_fusion), channel_id=1, replica_groups=mesh['groups'=2,'dom'=4,'mem'=2,'sub'=2] {'dom','mem','sub'}, use_global_device_ids=true, to_apply=%region_22.23 | all-reduce | flops 8192 | bytes 65536 | tf_op jit(solution)/shard_map/psum | solution.py:61
  420.4 47.0 %while.63 = (s32[]{:T(128)}, f32[16,4096]{1,0:T(8,128)S(1)}, f32[32,256]{1,0:T(8,128)S(1)}, f32[64,256]{1,0:T(8,128)S(1)}, f32[16,256]{1,0:T(8,128)S(1)}, /*inde...) while((s32[]{:T(128)}, f32[16,4096]{1,0:T(8,128)S(1)}, ...), condition=%wide.region_27.28_spmd, body=%wide.region_26.27_spmd.sunk | while | flops 75636760 | bytes 2466150 | solution.py:80
  (292 shorter events, 156.2 us)
Async XLA Ops:
  0.0 1.8 copy-start
  0.0 4.6 copy-start.2
  0.0 3.2 copy-start.1
  12.9 5.6 %copy-start.6 = (s32[64,16]{0,1:T(8,128)S(1)}, s32[64,16]{0,1:T(8,128)}, u32[]{:S(2)}) copy-start(s32[64,16]{0,1:T(8,128)} %param.23) | copy-start | bytes 12292
  12.9 5.6 %copy-start.4 = (s32[1024,4]{0,1:T(4,128)S(1)}, s32[1024,4]{0,1:T(4,128)}, u32[]{:S(2)}) copy-start(s32[1024,4]{0,1:T(4,128)} %param.17) | copy-start | bytes 49156
  20.5 3.2 copy-start.5
  467.4 0.7 copy-start.3
where the time goes:
time: 469 us; the launch traced here: 468 us
  blocking collectives  383 us (82%)
  local copies, waits for them, and re-layouts  41.1 us (9%)
  matrix products  37.3 us (8%)
    psum x4, blocking collectives, body(): obs_prior = lax.psum(padded, ('dom', 'mem', 'sub'))  236 us
    all_gather x32, blocking collectives, update(): all_members = lax.all_gather(cell_block, 'mem', axis=0, tiled=True)  147 us
    dot_general x32, matrix products, update(): jnp.einsum('mc,mp->cp', all_members, spread, precision=lax.Precision.HIGH...  19.8 us
    dot_general x32, matrix products, update(): jnp.einsum('mp,cp->mc', my_shift, gain_matrix, precision=lax.Precision.HI...  17.5 us
    gather x4, local copies, waits for them, and re-layouts, body(): current[:, spot_cells] * interp[None]  11.3 us

commit v1 on v0

v1 whole, which is shorter than its diff:
```python
import functools

import jax
import jax.numpy as jnp
from jax import lax
from jax.experimental import pallas as pl
from jax.experimental.pallas import tpu as pltpu
from jax.sharding import PartitionSpec as P

BLOCK = 64
P_SIZE = 256
NBATCH = 4
LANES = 128
CHUNK = 2048
F32 = jnp.float32
BF16 = jnp.bfloat16


def pieces(value, count):
    found = []
    for _ in range(count):
        head = value.astype(BF16).astype(F32)
        found.append(head)
        value = value - head
    return found


def halves(value):
    head = value.astype(BF16)
    return head, (value - head.astype(F32)).astype(BF16)


def dot(left, right):
    return lax.dot_general(left, right, (((1,), (0,)), ((), ())), preferred_element_type=F32)


def dot_first(left, right):
    return lax.dot_general(left, right, (((0,), (0,)), ((), ())), preferred_element_type=F32)


def kernel(
    sizes,
    x_ref, links_ref, cells_ref, owners_ref, interp_ref, order_ref, obs_ref, noise_ref,
    out_ref,
    everyone, link_slots, contrib, parts_in, priors, perm, links_t, hot_t, near_t,
    mask_st, mask_cells, stations, gains, shifts,
    x_send, x_recv, l_send, l_recv, r_send, r_recv, g_send, g_recv,
):
    nparts, nsub, nmem, nred = sizes
    rows, width = x_ref.shape
    blocks = width // BLOCK
    nblk = nparts * blocks
    members = rows * nmem
    nsta = order_ref.shape[1]
    piece = nsta // nred
    total = nparts * nmem
    part = lax.axis_index("dom") * nsub + lax.axis_index("sub")
    mem = lax.axis_index("mem")
    me = part * nmem + mem

    def place(which, member):
        return {"dom": which // nsub, "mem": member, "sub": which % nsub}

    def each(count, act):
        if count <= 16:
            for k in range(1, count):
                act(k)
        else:
            lax.fori_loop(1, count, lambda k, c: (act(k), c)[1], 0)

    def only(condition, act):
        if nred == nparts:
            act()
        else:
            pl.when(condition)(act)

    barrier = pltpu.get_barrier_semaphore()

    def greet(k):
        to = lax.rem(me + k, total)
        pl.semaphore_signal(
            barrier, inc=1, device_id=place(to // nmem, to % nmem),
            device_id_type=pl.DeviceIdType.MESH,
        )

    each(total, greet)
    pl.semaphore_wait(barrier, total - 1)

    my_rows = pl.ds(pl.multiple_of(mem * rows, rows), rows)

    def copy_x(k):
        return pltpu.make_async_remote_copy(
            src_ref=x_ref, dst_ref=everyone.at[my_rows, :],
            send_sem=x_send.at[k - 1], recv_sem=x_recv.at[k - 1],
            device_id=place(part, lax.rem(mem + k, nmem)),
            device_id_type=pl.DeviceIdType.MESH,
        )

    def copy_links(k):
        return pltpu.make_async_remote_copy(
            src_ref=links_ref, dst_ref=link_slots.at[part],
            send_sem=l_send.at[k - 1], recv_sem=l_recv.at[k - 1],
            device_id=place(lax.rem(part + k, nparts), mem),
            device_id_type=pl.DeviceIdType.MESH,
        )

    def copy_part(k):
        to = lax.rem(part + k, nparts)
        return pltpu.make_async_remote_copy(
            src_ref=contrib.at[lax.rem(to, nred)], dst_ref=parts_in.at[part],
            send_sem=r_send.at[k - 1], recv_sem=r_recv.at[k - 1],
            device_id=place(to, mem), device_id_type=pl.DeviceIdType.MESH,
        )

    def my_prior():
        column = pl.multiple_of(lax.rem(part, nred) * piece, piece)
        return priors.at[my_rows, pl.ds(column, piece)]

    def copy_prior(k):
        to = lax.rem(me + k, total)
        return pltpu.make_async_remote_copy(
            src_ref=my_prior(), dst_ref=my_prior(),
            send_sem=g_send.at[k - 1], recv_sem=g_recv.at[k - 1],
            device_id=place(to // nmem, to % nmem), device_id_type=pl.DeviceIdType.MESH,
        )

    each(nparts, lambda k: copy_links(k).start())
    each(nmem, lambda k: copy_x(k).start())

    cells = cells_ref[...]
    within = cells % LANES
    lane_of = lax.broadcasted_iota(jnp.int32, (LANES, nsta), 0)
    weights = jnp.zeros((LANES, nsta), F32)
    for k in range(cells.shape[0]):
        weights += jnp.where(lane_of == within[k : k + 1, :], interp_ref[k : k + 1, :], 0.0)
    w_hi, w_lo = halves(weights)
    tiles = width // LANES
    x_rows = jnp.concatenate(
        [x_ref[:, t * LANES : (t + 1) * LANES] for t in range(tiles)], axis=0
    )
    x_hi, x_lo = halves(x_rows)
    seen = dot(
        jnp.concatenate([x_hi, x_hi, x_lo], axis=1), jnp.concatenate([w_hi, w_lo, w_hi], axis=0)
    )
    owners = owners_ref[...]
    tile_of = (owners - part) * tiles + cells[0:1, :] // LANES
    share = jnp.zeros((rows, nsta), F32)
    for t in range(tiles):
        share += jnp.where(tile_of == t, seen[t * rows : (t + 1) * rows, :], 0.0)
    for r in range(nred):
        contrib[r] = share[:, r * piece : (r + 1) * piece]
    each(
        nparts,
        lambda k: only(lax.rem(part + k, nparts) < nred, lambda: copy_part(k).start()),
    )
    parts_in[part] = contrib[lax.rem(part, nred)]
    link_slots[part] = links_ref[...]
    everyone[my_rows, :] = x_ref[...]

    order = order_ref[...]
    strip = P_SIZE

    def build_perm(t, carry):
        first = pl.multiple_of(t * strip, strip)
        station = lax.broadcasted_iota(jnp.int32, (strip, nsta), 0) + first
        perm[pl.ds(first, strip), :] = (station == order).astype(F32).astype(BF16)
        return carry

    lax.fori_loop(0, nsta // strip, build_perm, 0)
    listed = jnp.concatenate(
        [owners.astype(F32), (cells[0:1, :] // BLOCK).astype(F32)]
        + pieces(obs_ref[...], 3)
        + pieces(noise_ref[...], 3),
        axis=0,
    )
    listed = dot(listed.astype(BF16), perm[...])
    station_block = (listed[0:1, :] * blocks + listed[1:2, :]).astype(jnp.int32)
    observed = listed[2:3, :] + listed[3:4, :] + listed[4:5, :]
    noise_var = listed[5:6, :] + listed[6:7, :] + listed[7:8, :]

    def reduce_shares():
        each(nparts, lambda k: copy_part(k).wait_recv())
        summed = parts_in[0]
        for q in range(1, nparts):
            summed += parts_in[q]
        my_prior()[...] = summed
        each(total, lambda k: copy_prior(k).start())

    only(part < nred, reduce_shares)
    each(
        nparts,
        lambda k: only(lax.rem(part + k, nparts) < nred, lambda: copy_part(k).wait_send()),
    )

    each(nparts, lambda k: copy_links(k).wait())
    all_links = jnp.concatenate([link_slots[q] for q in range(nparts)], axis=1)

    def build_links(t, carry):
        first = pl.multiple_of(t * BLOCK, BLOCK)
        block = lax.broadcasted_iota(jnp.int32, (BLOCK, nblk), 0) + first
        hit = block == all_links[0:1, :]
        for k in range(1, all_links.shape[0]):
            hit = hit | (block == all_links[k : k + 1, :])
        links_t[pl.ds(first, BLOCK), :] = hit.astype(F32).astype(BF16)
        block = lax.broadcasted_iota(jnp.int32, (BLOCK, nsta), 0) + first
        hot_t[pl.ds(first, BLOCK), :] = (block == station_block).astype(F32).astype(BF16)
        return carry

    lax.fori_loop(0, nparts, build_links, 0)
    local_block = lax.broadcasted_iota(jnp.int32, (blocks, width), 0)
    local_cell = lax.broadcasted_iota(jnp.int32, (blocks, width), 1)
    spread_out = (local_cell // BLOCK == local_block).astype(F32).astype(BF16)
    block_col = lax.broadcasted_iota(jnp.int32, (nblk, blocks), 0)
    block_row = lax.broadcasted_iota(jnp.int32, (nblk, blocks), 1)
    mine = (block_col == block_row + part * blocks).astype(F32).astype(BF16)
    for b in range(NBATCH):
        span = slice(b * P_SIZE, (b + 1) * P_SIZE)
        near = dot_first(hot_t[:, span], links_t[...]).astype(BF16)
        if b + 1 < NBATCH:
            mask_st[span, (b + 1) * P_SIZE :] = dot(near, hot_t[:, (b + 1) * P_SIZE :]).astype(BF16)
        near_t[span, :] = dot(near, mine).astype(BF16)

    def build_mask(t, carry):
        first = pl.multiple_of(t * P_SIZE, P_SIZE)
        near = near_t[pl.ds(first, P_SIZE), :]
        mask_cells[pl.ds(first, P_SIZE), :] = dot(near, spread_out).astype(BF16)
        return carry

    lax.fori_loop(0, NBATCH, build_mask, 0)

    def prior_sent(k):
        only(part < nred, lambda: copy_prior(k).wait_send())
        sender = lax.rem(me + total - k, total)
        only(sender // nmem < nred, lambda: copy_prior(k).wait_recv())

    each(total, prior_sent)
    ordered = dot(jnp.concatenate(pieces(priors[...], 3), axis=0).astype(BF16), perm[...])
    stations[...] = (
        ordered[:members] + ordered[members : 2 * members] + ordered[2 * members :]
    )

    def step(b, state, mask):
        high, low = halves(state)
        cross = dot(gains[b], jnp.concatenate([high, high, low], axis=0))
        c_hi, c_lo = halves(cross)
        shift = shifts[b]
        z_hi = c_hi * mask
        return state + dot(
            jnp.concatenate([shift[:members], shift[members:], shift[:members]], axis=1),
            jnp.concatenate([z_hi, z_hi, c_lo * mask], axis=0),
        )

    for b in range(NBATCH):
        span = slice(b * P_SIZE, (b + 1) * P_SIZE)
        prior = stations[:, span]
        noise_b, observed_b = noise_var[:, span], observed[:, span]
        mean = jnp.sum(prior, axis=0, keepdims=True) / members
        spread = prior - mean
        variance = jnp.sum(spread * spread, axis=0, keepdims=True) / (members - 1)
        ratio = jnp.sqrt(noise_b / (variance + noise_b))
        posterior = (noise_b * mean + variance * observed_b) / (variance + noise_b)
        shift = posterior - mean + (ratio - 1.0) * spread
        gain = spread / ((variance + 1e-05) * (members - 1))
        g_hi, g_lo = pieces(gain, 2)
        gains[b] = jnp.concatenate([g_hi, g_lo, g_hi], axis=0).T.astype(BF16)
        shifts[b] = jnp.concatenate(pieces(shift, 2), axis=0).astype(BF16)
        if b + 1 < NBATCH:
            later = slice((b + 1) * P_SIZE, nsta)
            stations[:, later] = step(b, stations[:, later], mask_st[span, later])

    each(nmem, lambda k: copy_x(k).wait())
    chunk = min(CHUNK, width)

    for b in range(NBATCH):

        def update(t, carry):
            columns = pl.ds(pl.multiple_of(t * chunk, chunk), chunk)
            mask = mask_cells[b * P_SIZE : (b + 1) * P_SIZE, columns]
            everyone[:, columns] = step(b, everyone[:, columns], mask)
            return carry

        lax.fori_loop(0, width // chunk, update, 0)
    out_ref[...] = everyone[my_rows, :]


def body(
    sizes, ensemble, station_cells, owners, interp_weights, station_order, obs_values, obs_var,
    partners,
):
    nparts, nsub, nmem, nred = sizes
    rows, width = ensemble.shape
    blocks, listed = partners.shape
    nsta = owners.shape[0]
    members, nblk, total = rows * nmem, nparts * blocks, nparts * nmem
    piece = nsta // nred
    dma = pltpu.SemaphoreType.DMA
    return pl.pallas_call(
        functools.partial(kernel, sizes),
        out_shape=jax.ShapeDtypeStruct((rows, width), F32),
        in_specs=[pl.BlockSpec(memory_space=pltpu.VMEM)] * 8,
        out_specs=pl.BlockSpec(memory_space=pltpu.VMEM),
        scratch_shapes=[
            pltpu.VMEM((members, width), F32),
            pltpu.VMEM((nparts, listed, blocks), jnp.int32),
            pltpu.VMEM((nred, rows, piece), F32),
            pltpu.VMEM((nparts, rows, piece), F32),
            pltpu.VMEM((members, nsta), F32),
            pltpu.VMEM((nsta, nsta), BF16),
            pltpu.VMEM((nblk, nblk), BF16),
            pltpu.VMEM((nblk, nsta), BF16),
            pltpu.VMEM((nsta, blocks), BF16),
            pltpu.VMEM((nsta, nsta), BF16),
            pltpu.VMEM((nsta, width), BF16),
            pltpu.VMEM((members, nsta), F32),
            pltpu.VMEM((NBATCH, P_SIZE, 3 * members), BF16),
            pltpu.VMEM((NBATCH, 2 * members, P_SIZE), BF16),
            dma((max(nmem - 1, 1),)),
            dma((max(nmem - 1, 1),)),
            dma((max(nparts - 1, 1),)),
            dma((max(nparts - 1, 1),)),
            dma((max(nparts - 1, 1),)),
            dma((max(nparts - 1, 1),)),
            dma((max(total - 1, 1),)),
            dma((max(total - 1, 1),)),
        ],
        compiler_params=pltpu.CompilerParams(
            collective_id=0, has_side_effects=True, vmem_limit_bytes=56 * 1024 * 1024
        ),
    )(
        ensemble, partners.T, station_cells.T, owners[None], interp_weights.T,
        station_order[None], obs_values[None], obs_var[None],
    )


def solution(mesh):
    nsub, nmem = mesh.shape["sub"], mesh.shape["mem"]
    nparts = mesh.shape["dom"] * nsub

    def local(*arrays):
        nred = min(nparts, arrays[2].shape[0] // LANES)
        return body((nparts, nsub, nmem, nred), *arrays)

    return jax.shard_map(
        local,
        mesh=mesh,
        in_specs=(
            P("mem", ("groups", "dom", "sub")),
            P("groups", None),
            P("groups"),
            P("groups", None),
            P("groups"),
            P("groups"),
            P("groups"),
            P(("groups", "dom", "sub"), None),
        ),
        out_specs=P("mem", ("groups", "dom", "sub")),
        check_vma=False,
    )
```

time: 469 us -> 30.5 us (0.07)
  blocking collectives: 383 us -> 0 us
  local copies, waits for them, and re-layouts: 41.1 us -> 1.67 us
  matrix products: 37.3 us -> 0 us
  Pallas kernels: 0 us -> 28.6 us
    psum x4 -> x0, blocking collectives: 236 us -> none  [body(): obs_prior = lax.psum(padded, ('dom', 'mem', 'sub'))]
    all_gather x32 -> x0, blocking collectives: 147 us -> none  [update(): all_members = lax.all_gather(cell_block, 'mem', axis=0, tiled=True)]
    dot_general x64 -> x0, matrix products: 37.3 us -> none  [the longest x32 19.8 us: update(): jnp.einsum('mc,mp->cp', all_members, spread, precision=lax.Precision.HIGH...]
    gather x24 -> x0, local copies, waits for them, and re-layouts: 33.5 us -> none  [the longest x4 11.3 us: body(): current[:, spot_cells] * interp[None]]
    pallas_call x0 -> x1, Pallas kernels: none -> 28.6 us  [body(): pl.pallas_call(functools.partial(kernel, sizes), out_shape=jax.ShapeDtype...]
where the time goes in v1:
time: 30.5 us; the launch traced here: 30.3 us
  Pallas kernels  28.6 us (94%)
  local copies, waits for them, and re-layouts  1.67 us (5%)
    pallas_call x1, Pallas kernels, body(): pl.pallas_call(functools.partial(kernel, sizes), out_shape=jax.ShapeDtype...  28.6 us
    unnamed x1, local copies, waits for them, and re-layouts  1.67 us

profile of v1, /device:TPU:0, one launch (start us, length us, event | category | flops | bytes accessed | tf_op | source)
XLA Modules:
  0.0 30.3 jit_solution(15821827427234074787)
XLA Ops:
  0.0 28.6 %shard_map.82 = f32[16,4096]{1,0:T(8,128)} custom-call(f32[16,4096]{1,0:T(8,128)} %x_ref.1, s32[16,64]{1,0:T(8,128)} %bitcast.9, s32[4,1024]{1,0:T(4,128)} %bitcast.7, s32[1,1024]{1,0:T(1,128)} %bitcast.10, f32[4,1024]{1,0:T(4,128)} %bitcast.8, s32[1,1024]{1,0:T(1,128)} %bitcast.11, f32[1,1024]{1,0:T(1,128)} %bitcast.12, f32[1,1024]{1,0:T(1,128)} %bitcast.13), custom_call_target="tpu_custom_call" | custom-call | tf_op jit(solution)/shard_map/pallas_call | solution.py:297
  28.6 1.7 %copy.10 = f32[16,4096]{1,0:T(8,128)} copy(f32[16,4096]{1,0:T(8,128)} %shard_map.82) | data formatting | bytes 524288

commit v2 on v1

--- a/solution.py
+++ b/solution.py
@@ -84,8 +84,6 @@
         )
 
     each(total, greet)
-    pl.semaphore_wait(barrier, total - 1)
-
     my_rows = pl.ds(pl.multiple_of(mem * rows, rows), rows)
 
     def copy_x(k):
@@ -123,9 +121,6 @@
             send_sem=g_send.at[k - 1], recv_sem=g_recv.at[k - 1],
             device_id=place(to // nmem, to % nmem), device_id_type=pl.DeviceIdType.MESH,
         )
-
-    each(nparts, lambda k: copy_links(k).start())
-    each(nmem, lambda k: copy_x(k).start())
 
     cells = cells_ref[...]
     within = cells % LANES
@@ -149,10 +144,13 @@
         share += jnp.where(tile_of == t, seen[t * rows : (t + 1) * rows, :], 0.0)
     for r in range(nred):
         contrib[r] = share[:, r * piece : (r + 1) * piece]
+    pl.semaphore_wait(barrier, total - 1)
     each(
         nparts,
         lambda k: only(lax.rem(part + k, nparts) < nred, lambda: copy_part(k).start()),
     )
+    each(nparts, lambda k: copy_links(k).start())
+    each(nmem, lambda k: copy_x(k).start())
     parts_in[part] = contrib[lax.rem(part, nred)]
     link_slots[part] = links_ref[...]
     everyone[my_rows, :] = x_ref[...]

time: 30.5 us -> 30.3 us (level)
  no operation moved by 1% of the time
where the time goes in v2:
time: 30.3 us; the launch traced here: 30.1 us
  Pallas kernels  28.4 us (94%)
  local copies, waits for them, and re-layouts  1.67 us (6%)
    pallas_call x1, Pallas kernels, body(): pl.pallas_call(functools.partial(kernel, sizes), out_shape=jax.ShapeDtype...  28.4 us
    unnamed x1, local copies, waits for them, and re-layouts  1.67 us

profile of v2, /device:TPU:0, one launch (start us, length us, event | category | flops | bytes accessed | tf_op | source)
XLA Modules:
  0.0 30.1 jit_solution(1496927590265132517)
XLA Ops:
  0.0 28.4 %shard_map.82 = f32[16,4096]{1,0:T(8,128)} custom-call(f32[16,4096]{1,0:T(8,128)} %x_ref.1, s32[16,64]{1,0:T(8,128)} %bitcast.9, s32[4,1024]{1,0:T(4,128)} %bitcast.7, s32[1,1024]{1,0:T(1,128)} %bitcast.10, f32[4,1024]{1,0:T(4,128)} %bitcast.8, s32[1,1024]{1,0:T(1,128)} %bitcast.11, f32[1,1024]{1,0:T(1,128)} %bitcast.12, f32[1,1024]{1,0:T(1,128)} %bitcast.13), custom_call_target="tpu_custom_call" | custom-call | tf_op jit(solution)/shard_map/pallas_call | solution.py:295
  28.4 1.7 %copy.10 = f32[16,4096]{1,0:T(8,128)} copy(f32[16,4096]{1,0:T(8,128)} %shard_map.82) | data formatting | bytes 524288
